TPU v7x, 32 devices: a whole 2x2x4 slice. The times are simulated.
32 devices in a mesh: groups: 2 (over x), exp: 16 (over z, y, core).
Axes of the slice: x: 2, y: 2, z: 4, core: 2. Of those that a mesh axis runs over, the one named last changes fastest.
Arguments:
- estimate: float32 [512, 4, 512], P('exp', 'groups'), parts along dimension 1, may hold values from -6 to 6
- observed: bfloat16 [32, 512, 512], P(('groups', 'exp')), parts along dimension 0, may hold values from -12 to 12
- pixel_mask: int32 [32, 512, 512], P(('groups', 'exp')), parts along dimension 0, may hold values 0 or 1
- blur_mix: float32 [32, 6, 8, 8], P(('groups', 'exp')), parts along dimension 0, may hold values from 0.2 to 1
- dithers: int32 [32, 2], P(('groups', 'exp')), parts along dimension 0, may hold values from -8 to 8, as said below
- patch_of: int32 [32], P(('groups', 'exp')), parts along dimension 0, may hold values from 0 to 1
- column_taps: bfloat16 [6, 15], replicated, may hold values from 0 to 0.119628906
- row_taps: bfloat16 [6, 15], replicated, may hold values from 0 to 0.119628906
Outputs:
- gradient: float32 [512, 4, 512], P('exp', 'groups'), parts along dimension 1
There are 2 independent parts, one for each index of `groups`. A program takes and returns all parts, laid end to end along the dimension named above; an argument that names none is the same for every part. Nothing has to cross between parts.
Inputs may be any that keep to these rules, and one draw needn't show every extreme that they name: `dithers`: each exposure's two offsets; the value 8 occurs among the row offsets and -8 among the column offsets.
All inputs are finite; a program needn't handle non-finite values. No bound on the sum of `pixel_mask` on one device may be relied on, other than what follows from the above.
Results may differ from a plain program's by a relative error of at most 0.004.
Values may be sent and summed in bfloat16 or wider, within the bound.
A program may use at most 128 MiB of HBM per device.

v0:
```python
import jax
import jax.numpy as jnp
from jax import lax
from jax.sharding import PartitionSpec as P

DMAX = 8


def band_stack(tap_values, extent, col_offset):
    half_width = tap_values.shape[1] // 2
    source = lax.broadcasted_iota(jnp.int32, (extent, extent), 0)
    target = lax.broadcasted_iota(jnp.int32, (extent, extent), 1)
    offset = source - target - col_offset + half_width
    inside = (source - col_offset >= 0) & (source - col_offset < extent)
    running = jnp.zeros((tap_values.shape[0], extent, extent), jnp.float32)
    for tap_index in range(tap_values.shape[1]):
        matches = ((offset == tap_index) & inside).astype(jnp.float32)
        running = (
            running + tap_values[:, tap_index].astype(jnp.float32)[:, None, None] * matches[None]
        )
    return running.astype(jnp.bfloat16)


def exposure_back(rowed, frame_data, mask_frame, blur_weights, row_shift, column_band):
    extent = frame_data.shape[0]
    basis_count = blur_weights.shape[0]
    tile_count = blur_weights.shape[1]
    tile_side = extent // tile_count
    padded = jnp.pad(rowed, ((DMAX, DMAX), (0, 0)))
    shifted = lax.dynamic_slice_in_dim(padded, DMAX + row_shift, extent, 0).reshape(
        extent, basis_count, extent
    )
    blurred = jnp.einsum("kba,bkc->kac", column_band, shifted, preferred_element_type=jnp.float32)
    mix_full = jnp.broadcast_to(
        blur_weights[:, :, None, :, None],
        (basis_count, tile_count, tile_side, tile_count, tile_side),
    ).reshape(basis_count, extent, extent)
    model_image = jnp.sum(mix_full * blurred, axis=0)
    residual = mask_frame.astype(jnp.float32) * (model_image - frame_data.astype(jnp.float32))
    weighted = (mix_full * residual[None]).astype(jnp.bfloat16)
    backed = jnp.einsum("kab,kbc->akc", column_band, weighted, preferred_element_type=jnp.float32)
    backed = backed.astype(jnp.bfloat16).reshape(extent, basis_count * extent)
    return jnp.pad(backed, ((DMAX, DMAX), (0, 0)))


def back_rows(padded_back, back_stack, row_shift, patch_index, patch_count, first_row, row_count):
    picked = lax.dynamic_slice_in_dim(padded_back, first_row + DMAX - row_shift, row_count, 0)
    result = jnp.dot(picked, back_stack, preferred_element_type=jnp.float32)
    selector = lax.broadcasted_iota(jnp.int32, (1, patch_count, 1), 1) == patch_index
    return jnp.where(selector, result[:, None, :], jnp.zeros((), jnp.float32))


def per_device(estimate, observed, pixel_mask, blur_mix, dithers, patch_of, column_taps, row_taps):
    extent = observed.shape[1]
    patch_count = estimate.shape[1]
    band_rows = estimate.shape[0]
    row_shift = dithers[0, 0]
    column_shift = dithers[0, 1]
    patch_index = patch_of[0]
    column_band = band_stack(column_taps, extent, 0)
    row_band = band_stack(row_taps, extent, column_shift)
    forward_stack = jnp.transpose(row_band, (1, 0, 2)).reshape(extent, -1)
    back_stack = jnp.transpose(row_band, (0, 2, 1)).reshape(-1, extent)
    estimate_low = estimate.astype(jnp.bfloat16)
    gathered = lax.all_gather(estimate_low, "exp", axis=0, tiled=True)
    chosen = lax.dynamic_index_in_dim(gathered, patch_index, 1, keepdims=False)
    rowed = jnp.dot(chosen, forward_stack, preferred_element_type=jnp.float32).astype(jnp.bfloat16)
    padded_back = exposure_back(
        rowed, observed[0], pixel_mask[0], blur_mix[0], row_shift, column_band
    )
    complete = lax.psum(
        back_rows(padded_back, back_stack, row_shift, patch_index, patch_count, 0, extent), "exp"
    )
    return lax.dynamic_slice_in_dim(complete, lax.axis_index("exp") * band_rows, band_rows, 0)


def solution(mesh):
    in_specs = (
        P("exp", "groups", None),
        P(("groups", "exp"), None, None),
        P(("groups", "exp"), None, None),
        P(("groups", "exp"), None, None, None),
        P(("groups", "exp"), None),
        P(("groups", "exp")),
        P(),
        P(),
    )
    out_specs = P("exp", "groups", None)
    return jax.shard_map(
        per_device, mesh=mesh, in_specs=in_specs, out_specs=out_specs, check_vma=False
    )
```

profile of v0, /device:TPU:0, one launch (start us, length us, event | category | flops | bytes accessed | tf_op | source)
XLA Modules:
  0.0 286.6 jit_solution(5062200893745384783)
XLA Ops:
  6.5 1.6 copy.50
  8.2 1.4 fusion.165
  9.6 0.7 fusion.161
  10.3 7.4 %fusion.68 = (f32[512,512]{0,1:T(8,128)S(1)}, f32[512,512]{0,1:T(8,128)}, f32[512,512]{0,1:T(8,128)S(1)}, f32[512,512]{0,1:T(8,128)S(1)}, f32[512,512]{0,1:T(8,1...) fusion(s32[]{:T(128)} %bitcast.3, ...), kind=kLoop, calls=%fused_computation.95 | loop fusion | flops 25165824 | bytes 31457796 | tf_op jit(solution)/shard_map/convert_element_type | solution.py:17
  17.7 0.3 convert_reduce_fusion.14
  18.0 8.4 %add_convert_fusion = bf16[512,6,512]{0,2,1:T(8,128)(2,1)} fusion(f32[512,512]{0,1:T(8,128)S(1)} %get-tuple-element.51, f32[6]{0:T(128)S(1)} %get-tuple-element.33, f32[512,512]{0,1:T(8,128)S(1)} %get-tuple-element.52, f32[6]{0:T(128)S(1)} %get-tuple-element.34, f32[512,512]{0,1:T(8,128)S(1)} %get-tuple-element.53, f32[6]{0:T(128)S(1)} %get-tuple-element.21, ...), kind=kLoop, calls=%fused_computation.32 | loop fusion | flops 47185920 | bytes 18874728 | tf_op jit(solution)/shard_map/convert_element_type | solution.py:21
  26.4 7.0 %fusion.128 = (f32[512,512]{0,1:T(8,128)}, f32[512,512]{0,1:T(8,128)}, f32[512,512]{0,1:T(8,128)}, f32[512,512]{0,1:T(8,128)}, f32[512,512]{0,1:T(8,128)}, /*ind...) fusion(pred[512]{0:T(512)(128)(4,1)S(1)} %iota_compare_fusion), kind=kLoop, calls=%fused_computation.155 | loop fusion | flops 12320768 | bytes 15729152 | tf_op jit(solution)/shard_map/convert_element_type | solution.py:17
  36.3 2.5 copy.11
  38.8 2.6 copy.12
  41.4 2.5 copy.13
  44.0 2.6 copy.14
  46.5 2.5 copy.15
  49.0 2.5 copy.16
  51.6 2.6 copy.17
  54.1 2.5 copy.18
  56.7 2.6 copy.19
  59.3 2.5 copy.20
  61.8 2.5 copy.21
  64.3 2.6 copy.22
  66.9 2.6 copy.23
  69.5 2.5 copy.24
  72.0 2.5 copy.25
  74.6 5.4 %broadcast_in_dim.19 = f32[6,8,64,8,64]{4,3,2,1,0:T(8,128)} broadcast(f32[6,8,8]{2,1,0:T(8,128)S(1)} %bitcast.127), dimensions={0,1,3} | broadcast | bytes 6292992 | tf_op jit(solution)/shard_map/broadcast_in_dim | solution.py:34
  80.0 11.5 %reshape.1297 = f32[6,512,512]{2,1,0:T(8,128)} reshape(f32[6,8,64,8,64]{4,3,2,1,0:T(8,128)} %broadcast_in_dim.19) | data formatting | bytes 12582912 | tf_op jit(solution)/shard_map/reshape | solution.py:37
  91.5 2.5 copy.31
  94.1 2.6 copy.32
  96.7 2.5 copy.33
  99.2 2.5 copy.34
  101.7 2.6 copy.35
  104.3 2.6 copy.36
  106.9 2.6 copy.37
  109.4 2.5 copy.38
  112.0 2.5 copy.39
  114.5 2.5 copy.40
  117.0 2.6 copy.41
  119.6 2.5 copy.42
  122.2 1.3 copy.43
  123.5 0.3 copy.44
  123.9 0.3 copy.45
  124.2 0.1 mul.850
  124.3 0.1 mul.856
  124.3 0.1 mul.862
  124.4 0.1 mul.868
  124.5 0.1 mul.874
  124.6 0.1 mul.880
  124.7 0.1 mul.886
  124.7 0.1 mul.892
  124.8 0.1 mul.898
  125.1 0.1 mul.922
  125.2 0.1 mul.928
  125.3 0.1 mul.934
  125.4 12.8 %fusion.1 = bf16[3072,512]{1,0:T(8,128)(2,1)} fusion(f32[512,512]{1,0:T(8,128)S(1)} %copy.45, f32[3072]{0:T(1024)S(1)} %mul.935, f32[512,512]{1,0:T(8,128)S(1)} %copy.44, f32[3072]{0:T(1024)S(1)} %mul.929, f32[512,512]{1,0:T(8,128)} %copy.43, f32[3072]{0:T(1024)S(1)} %mul.923, f32[512,512]{1,0:T(8,128)} %copy.42, f32[3072]{0:T(1024)S(1)} %mul.917, ...), kind=kLoop, calls=%fused_computation.2 | loop fusion | flops 47185920 | bytes 19058688 | tf_op jit(solution)/shard_map/convert_element_type | solution.py:21
  138.2 0.3 convert_reduce_fusion.29
  138.5 10.5 %add_convert_fusion.1 = bf16[6,512,512]{2,1,0:T(8,128)(2,1)S(1)} fusion(f32[512,512]{1,0:T(8,128)} %copy.25, f32[6]{0:T(128)S(1)} %get-tuple-element.18, f32[512,512]{1,0:T(8,128)} %copy.24, f32[6]{0:T(128)S(1)} %get-tuple-element.19, f32[512,512]{1,0:T(8,128)} %copy.23, f32[6]{0:T(128)S(1)} %get-tuple-element.6, f32[512,512]{1,0:T(8,128)} %copy.22, ...), kind=kLoop, calls=%fused_computation.33 | loop fusion | flops 47185920 | bytes 18874728 | tf_op jit(solution)/shard_map/convert_element_type | solution.py:21
  149.1 3.9 %convolution_convert_fusion = bf16[512,3072]{1,0:T(8,128)(2,1)S(1)} fusion(bf16[512,3072]{0,1:T(8,128)(2,1)} %bitcast.125, bf16[512,2,512]{2,0,1:T(8,128)(2,1)} %all-gather.2.cloned.1.call-done, s32[]{:T(128)S(6)} %select_n.17), kind=kOutput, calls=%fused_computation.34 | convolution fusion | flops 1612185600 | bytes 6815748 | tf_op jit(solution)/shard_map/dot_general | solution.py:67
  153.0 2.5 pad_dynamic-slice_fusion.1
  155.5 4.7 %copy.27 = bf16[512,3072]{0,1:T(8,128)(2,1)} copy(bf16[512,3072]{1,0:T(8,128)(2,1)} %pad_dynamic-slice_fusion.1) | data formatting | bytes 6291456 | tf_op jit(solution)/shard_map/dynamic_slice | solution.py:30
  160.3 6.2 %multiply_reduce_fusion = f32[512,512]{1,0:T(8,128)S(1)} fusion(f32[6,512,512]{2,1,0:T(8,128)} %reshape.1297, bf16[6,512,512]{2,1,0:T(8,128)(2,1)S(1)} %add_convert_fusion.1, bf16[512,6,512]{0,2,1:T(8,128)(2,1)} %bitcast.124), kind=kOutput, calls=%fused_computation.31 | convolution fusion | flops 1613496320 | bytes 13631488 | tf_op jit(solution)/shard_map/kba,bkc->kac/dot_general | solution.py:33
  166.5 0.3 fusion.20
  166.8 4.0 %fusion.18 = bf16[6,512,512]{2,1,0:T(8,128)(2,1)} fusion(bf16[6,512,512]{2,1,0:T(8,128)(2,1)S(1)} %add_convert_fusion.1, f32[6,512,512]{2,1,0:T(8,128)S(1)} %bitcast.123, f32[512,512]{1,0:T(8,128)S(1)} %fusion.20), kind=kOutput, calls=%fused_computation.40 | convolution fusion | flops 1615331328 | bytes 13631488 | tf_op jit(solution)/shard_map/kab,kbc->akc/dot_general | solution.py:41
  170.8 4.5 %fusion.15 = f32[512,512]{1,0:T(8,128)S(1)} fusion(bf16[3072,512]{1,0:T(8,128)(2,1)S(1)} %copy-done, s32[]{:T(128)S(6)} %select_n.19, bf16[512,3072]{0,1:T(8,128)(2,1)} %bitcast.126), kind=kOutput, calls=%fused_computation.37 | convolution fusion | flops 1610612736 | bytes 7340036 | tf_op jit(solution)/shard_map/dot_general | solution.py:48
  175.3 2.3 broadcast_select_fusion
  177.6 100.6 %all-reduce.4.cloned.1.call-done = f32[512,2,512]{2,1,0:T(2,128)} async-done(((f32[512,2,512]{2,1,0:T(2,128)}), f32[512,2,512]{2,1,0:T(2,128)}) %all-reduce.4.cloned.1.call-update) | async-done | bytes 2097168 | tf_op jit(solution)/shard_map/psum | solution.py:71
  278.2 1.6 constant_dynamic-slice_fusion
  (42 shorter events, 0.4 us)
Async XLA Ops:
  6.5 142.6 %all-gather.2.cloned.1.call-start = ((), (), s32[]{:S(2)}) async-start(), calls=%async_computation | async-start | bytes 1114112 | tf_op jit(solution)/shard_map/all_gather | solution.py:65
  8.1 270.1 %all-reduce.4.cloned.1.call-start = ((), (), s32[]{:S(2)}) async-start(), calls=%async_computation.1 | async-start | bytes 4194304 | tf_op jit(solution)/shard_map/psum | solution.py:71
  10.2 7.5 %copy-start.3 = (bf16[6,15]{1,0:T(8,128)(2,1)S(1)}, bf16[6,15]{1,0:T(8,128)(2,1)}, u32[]{:S(2)}) copy-start(bf16[6,15]{1,0:T(8,128)(2,1)} %param.15) | copy-start | bytes 544
  59.3 15.3 %copy-start.5 = (f32[1,6,8,8]{3,2,1,0:T(8,128)S(1)}, f32[1,6,8,8]{3,2,1,0:T(8,128)}, u32[]{:S(2)}) copy-start(f32[1,6,8,8]{3,2,1,0:T(8,128)} %param.11) | copy-start | bytes 4612
  125.3 12.9 %copy-start.4 = (bf16[6,15]{1,0:T(8,128)(2,1)S(1)}, bf16[6,15]{1,0:T(8,128)(2,1)}, u32[]{:S(2)}) copy-start(bf16[6,15]{1,0:T(8,128)(2,1)} %param.14) | copy-start | bytes 544
  160.3 6.5 %slice-start = ((s8[6291456]{0:T(1024)(128)(4,1)}), s8[4194304]{0:T(1024)(128)(4,1)S(1)}, s32[]{:S(2)}) async-start(s8[6291456]{0:T(1024)(128)(4,1)} %bitcast.122), calls=%async_computation.2 | async-start | bytes 8388608
  160.3 6.2 %copy-start.1 = (s32[1,512,512]{2,1,0:T(8,128)S(1)}, s32[1,512,512]{2,1,0:T(8,128)}, u32[]{:S(2)}) copy-start(s32[1,512,512]{2,1,0:T(8,128)} %param.10) | copy-start | bytes 3145732
  160.3 6.2 %copy-start.2 = (bf16[1,512,512]{2,1,0:T(8,128)(2,1)S(1)}, bf16[1,512,512]{2,1,0:T(8,128)(2,1)}, u32[]{:S(2)}) copy-start(bf16[1,512,512]{2,1,0:T(8,128)(2,1)} %param.9) | copy-start | bytes 1572868
  160.3 6.5 %slice-start.1 = ((s8[6291456]{0:T(1024)(128)(4,1)}), s8[2097152]{0:T(1024)(128)(4,1)S(1)}, s32[]{:S(2)}) async-start(s8[6291456]{0:T(1024)(128)(4,1)} %bitcast.122), calls=%async_computation.3 | async-start | bytes 4194304
  166.8 4.0 %copy-start = (bf16[3072,512]{1,0:T(8,128)(2,1)S(1)}, bf16[3072,512]{1,0:T(8,128)(2,1)}, u32[]{:S(2)}) copy-start(bf16[3072,512]{1,0:T(8,128)(2,1)} %fusion.1) | copy-start | bytes 9437188
Sparse Core Ops, SparseCore 0:
  9.5 40.6 all-gather.1
  177.7 100.4 all-reduce.3
where the time goes:
time: 288 us; the launch traced here: 287 us
  local copies, waits for them, and re-layouts  101 us (35%)
  waiting for transfers between devices  101 us (35%)
  other arithmetic  50.1 us (17%)
  matrix products  18.5 us (6%)
  between operations  16.5 us (6%)
    psum x1, waiting for transfers between devices, per_device(): lax.psum(back_rows(padded_back, back_stack, row_shift, patch_index, patch...  101 us
    convert_element_type x30, local copies, waits for them, and re-layouts, band_stack(): matches = ((offset == tap_index) & inside).astype(jnp.float32)  70.9 us
    convert_element_type x3, other arithmetic, band_stack(): return running.astype(jnp.bfloat16)  31.8 us
    convert_element_type x2, other arithmetic, band_stack(): matches = ((offset == tap_index) & inside).astype(jnp.float32)  14.4 us
    reshape x1, local copies, waits for them, and re-layouts, exposure_back(): mix_full = jnp.broadcast_to(blur_weights[:, :, None, :, None], (basis_cou...  11.5 us
    dynamic_slice x2, local copies, waits for them, and re-layouts, exposure_back(): lax.dynamic_slice_in_dim(padded, DMAX + row_shift, extent, 0)  7.27 us
    dot_general x1, matrix products, exposure_back(): jnp.einsum('kba,bkc->kac', column_band, shifted, preferred_element_type=j...  6.17 us
  transfers between devices with their start and end apart: 2, of which 1 were waited for; matrix products, arithmetic and copies ran while one was open for 48% of the time, Pallas kernels for 0%

commit v1 on v0

v1 whole, which is shorter than its diff:
```python
import functools

import jax
import jax.numpy as jnp
from jax import lax
from jax.experimental import pallas as pl
from jax.experimental.pallas import tpu as pltpu
from jax.sharding import PartitionSpec as P

BLOCK = 128
EDGE = 16
F32 = jnp.float32
BF16 = jnp.bfloat16


def dot(a, b):
    return jnp.dot(a, b, preferred_element_type=F32)


def build_bands(taps_ref, plain_ref, flipped_ref):
    taps = taps_ref[...].astype(F32)
    bases, width = taps.shape
    half = width // 2
    extent = plain_ref.shape[1]
    blocks = extent // BLOCK
    zero = jnp.zeros((extent, extent), plain_ref.dtype)
    for k in range(bases):
        plain_ref[k] = zero
        flipped_ref[k] = zero

    for first, rows, shift in ((0, BLOCK, 0), (0, EDGE, -1), (BLOCK - EDGE, EDGE, 1)):
        shape = (rows, BLOCK)
        offset = (
            lax.broadcasted_iota(jnp.int32, shape, 0)
            + first
            - lax.broadcasted_iota(jnp.int32, shape, 1)
            - shift * BLOCK
            + half
        )
        plain = [jnp.zeros(shape, F32) for _ in range(bases)]
        flipped = [jnp.zeros(shape, F32) for _ in range(bases)]
        for t in range(width):
            match = offset == t
            for k in range(bases):
                plain[k] = jnp.where(match, taps[k : k + 1, t : t + 1], plain[k])
                other = width - 1 - t
                flipped[k] = jnp.where(match, taps[k : k + 1, other : other + 1], flipped[k])
        for k in range(bases):
            plain_block = plain[k].astype(BF16)
            flipped_block = flipped[k].astype(BF16)
            for block in range(blocks):
                if 0 <= block + shift < blocks:
                    at = (
                        k,
                        pl.ds(block * BLOCK + first, rows),
                        pl.ds((block + shift) * BLOCK, BLOCK),
                    )
                    plain_ref[at] = plain_block
                    flipped_ref[at] = flipped_block


def spread_mix(mix_ref, spread_ref):
    _, bases, tiles, _ = mix_ref.shape
    extent = spread_ref.shape[2]
    lane_tile = lax.broadcasted_iota(jnp.int32, (tiles, extent), 1) // (extent // tiles)
    for k in range(bases):
        weights = mix_ref[0, k]
        spread = jnp.zeros((tiles, extent), F32)
        for tile in range(tiles):
            spread = jnp.where(lane_tile == tile, weights[:, tile : tile + 1], spread)
        spread_ref[k] = spread


def mix_full(spread_ref, k):
    tiles, extent = spread_ref.shape[1:]
    weights = spread_ref[k]
    return jnp.broadcast_to(weights[:, None, :], (tiles, extent // tiles, extent)).reshape(
        extent, extent
    )


def one_hot(extent, shift):
    row = lax.broadcasted_iota(jnp.int32, (extent, extent), 0)
    column = lax.broadcasted_iota(jnp.int32, (extent, extent), 1)
    return jnp.where(column == row + shift, 1.0, 0.0).astype(BF16)


def exposure_term(
    chosen, shifts, observed_ref, mask_ref, spread_ref, bands, rowed_ref, model_ref, total_ref
):
    row_band, row_flip, column_band, column_flip = bands
    bases, extent, _ = row_band.shape
    row_shift, column_shift = shifts
    moved = dot(one_hot(extent, row_shift), chosen).astype(BF16)
    moved = dot(moved, one_hot(extent, -column_shift)).astype(BF16)
    rowed_ref[...] = moved
    model_ref[...] = jnp.zeros_like(model_ref)

    def forward(k, _):
        rowed = dot(rowed_ref[...], row_band[k]).astype(BF16)
        model_ref[...] += mix_full(spread_ref, k) * dot(column_flip[k], rowed)
        return 0

    lax.fori_loop(0, bases, forward, 0)
    model_ref[...] = mask_ref[0].astype(F32) * (model_ref[...] - observed_ref[0].astype(F32))
    total_ref[...] = jnp.zeros_like(total_ref)

    def backward(k, _):
        weighted = (mix_full(spread_ref, k) * model_ref[...]).astype(BF16)
        backed = dot(column_band[k], weighted).astype(BF16)
        total_ref[...] += dot(backed, row_flip[k])
        return 0

    lax.fori_loop(0, bases, backward, 0)
    back = dot(one_hot(extent, -row_shift), total_ref[...].astype(BF16)).astype(BF16)
    return dot(back, one_hot(extent, column_shift))


def local_kernel(
    dithers, patch_of, estimate, observed, mask, mix, column_taps, row_taps, term,
    row_band, row_flip, column_band, column_flip, spread, rowed, model, total,
):
    build_bands(row_taps, row_band, row_flip)
    build_bands(column_taps, column_band, column_flip)
    spread_mix(mix, spread)
    patch = patch_of[0]
    result = exposure_term(
        estimate[patch], (dithers[0, 0], dithers[0, 1]), observed, mask, spread,
        (row_band, row_flip, column_band, column_flip), rowed, model, total,
    )
    for q in range(term.shape[0]):
        term[q] = jnp.where(patch == q, result, 0.0)


def work_shapes(bases, tiles, extent):
    return [pltpu.VMEM((bases, extent, extent), BF16) for _ in range(4)] + [
        pltpu.VMEM((bases, tiles, extent), F32),
        pltpu.VMEM((extent, extent), BF16),
        pltpu.VMEM((extent, extent), F32),
        pltpu.VMEM((extent, extent), F32),
    ]


def per_device(estimate, observed, pixel_mask, blur_mix, dithers, patch_of, column_taps, row_taps):
    extent = observed.shape[1]
    patches = estimate.shape[1]
    bases, tiles = blur_mix.shape[1:3]
    vmem = pl.BlockSpec(memory_space=pltpu.VMEM)
    smem = pl.BlockSpec(memory_space=pltpu.SMEM)
    low = jnp.transpose(estimate.astype(BF16), (1, 0, 2))
    gathered = lax.all_gather(low, "exp", axis=1, tiled=True)
    term = pl.pallas_call(
        local_kernel,
        out_shape=jax.ShapeDtypeStruct((patches, extent, extent), F32),
        in_specs=[smem, smem] + [vmem] * 6,
        out_specs=vmem,
        scratch_shapes=work_shapes(bases, tiles, extent),
        compiler_params=pltpu.CompilerParams(vmem_limit_bytes=56 * 2**20),
    )(dithers, patch_of, gathered, observed, pixel_mask, blur_mix, column_taps, row_taps)
    mine = lax.psum_scatter(term, "exp", scatter_dimension=1, tiled=True)
    return jnp.transpose(mine, (1, 0, 2))


def solution(mesh):
    in_specs = (
        P("exp", "groups", None),
        P(("groups", "exp"), None, None),
        P(("groups", "exp"), None, None),
        P(("groups", "exp"), None, None, None),
        P(("groups", "exp"), None),
        P(("groups", "exp")),
        P(),
        P(),
    )
    return jax.shard_map(
        per_device,
        mesh=mesh,
        in_specs=in_specs,
        out_specs=P("exp", "groups", None),
        check_vma=False,
    )
```

time: 288 us -> 136 us (0.47)
  local copies, waits for them, and re-layouts: 101 us -> 3.22 us
  other arithmetic: 50.1 us -> 0 us
  matrix products: 18.5 us -> 0 us
  Pallas kernels: 0 us -> 16.5 us
    psum x1 -> x0, waiting for transfers between devices: 101 us -> none  [per_device(): lax.psum(back_rows(padded_back, back_stack, row_shift, patch_index, patch...]
    convert_element_type x30 -> x0, local copies, waits for them, and re-layouts: 70.9 us -> none  [band_stack(): matches = ((offset == tap_index) & inside).astype(jnp.float32)]
    reduce_scatter x0 -> x1, waiting for transfers between devices: none -> 60.6 us  [per_device(): mine = lax.psum_scatter(term, 'exp', scatter_dimension=1, tiled=True)]
    convert_element_type x7 -> x0, other arithmetic: 46.9 us -> none  [the longest x3 31.8 us: band_stack(): return running.astype(jnp.bfloat16)]
    all_gather x1, waiting for transfers between devices: 0.02 us -> 41.4 us  [per_device(): gathered = lax.all_gather(low, 'exp', axis=1, tiled=True)]
    dot_general x4 -> x0, matrix products: 18.5 us -> none  [the longest x1 6.17 us: exposure_back(): jnp.einsum('kba,bkc->kac', column_band, shifted, preferred_element_type=j...]
    pallas_call x0 -> x1, Pallas kernels: none -> 16.5 us  [per_device(): pl.pallas_call(local_kernel, out_shape=jax.ShapeDtypeStruct((patches, ext...]
    reshape x1 -> x0, local copies, waits for them, and re-layouts: 11.5 us -> none  [exposure_back(): mix_full = jnp.broadcast_to(blur_weights[:, :, None, :, None], (basis_cou...]
  transfers between devices with their start and end apart: 2 -> 2, of which waited for: 1 -> 2; matrix products, arithmetic and copies ran while one was open for 48% -> 0% of each run, Pallas kernels for 0% -> 0%
where the time goes in v1:
time: 136 us
  waiting for transfers between devices  102 us (75%)
  Pallas kernels  16.5 us (12%)
  between operations  14 us (10%)
  local copies, waits for them, and re-layouts  3.22 us (2%)
    reduce_scatter x1, waiting for transfers between devices, per_device(): mine = lax.psum_scatter(term, 'exp', scatter_dimension=1, tiled=True)  60.6 us
    all_gather x1, waiting for transfers between devices, per_device(): gathered = lax.all_gather(low, 'exp', axis=1, tiled=True)  41.4 us
    pallas_call x1, Pallas kernels, per_device(): pl.pallas_call(local_kernel, out_shape=jax.ShapeDtypeStruct((patches, ext...  16.5 us
  transfers between devices with their start and end apart: 2, of which 2 were waited for; matrix products, arithmetic and copies ran while one was open for 0% of the time, Pallas kernels for 0%

profile of v1, /device:TPU:0, one launch (start us, length us, event | category | flops | bytes accessed | tf_op | source)
XLA Modules:
  0.0 135.9 jit_solution(14733827485608946235)
XLA Ops:
  6.5 0.0 all-gather.2.cloned.1.call-start
  6.5 1.6 %copy.14 = bf16[32,2,512]{2,0,1:T(8,128)(2,1)} copy(f32[32,2,512]{2,1,0:T(2,128)} %param.8) | data formatting | bytes 196608 | tf_op args[0]
  8.1 0.0 all-gather.2.cloned.1.call-update
  8.1 0.0 reduce-scatter.2.cloned.1.call-start
  8.8 41.4 %all-gather.2.cloned.1.call-done.estimate = bf16[2,512,512]{2,1,0:T(8,128)(2,1)} async-done(((bf16[2,32,512]{2,1,0:T(8,128)(2,1)}), bf16[2,512,512]{2,1,0:T(8,128)(2,1)}) %all-gather.2.cloned.1.call-update) | async-done | bytes 1048592 | tf_op jit(solution)/shard_map/all_gather | solution.py:151
  50.2 16.5 %shard_map.82 = f32[2,512,512]{2,1,0:T(8,128)} custom-call(s32[1,2]{1,0:T(1,128)} %dithers.1, s32[1]{0:T(128)S(6)} %copy.15.patch_of, bf16[2,512,512]{2,1,0:T(8,128)(2,1)} %all-gather.2.cloned.1.call-done.estimate, bf16[1,512,512]{2,1,0:T(8,128)(2,1)} %observed.1, s32[1,512,512]{2,1,0:T(8,128)} %mask.1, f32[1,6,8,8]{3,2,1,0:T(8,128)} %mix.1, ...), custom_call_target="tpu_custom_call" | custom-call | tf_op jit(solution)/shard_map/pallas_call | solution.py:152
  66.7 0.0 reduce-scatter.2.cloned.1.call-update
  66.8 60.6 %reduce-scatter.2.cloned.1.call-done = f32[2,32,512]{2,1,0:T(8,128)} async-done(((f32[2,512,512]{2,1,0:T(8,128)}), f32[2,32,512]{2,1,0:T(8,128)}) %reduce-scatter.2.cloned.1.call-update) | async-done | bytes 131088 | tf_op jit(solution)/shard_map/reduce_scatter | solution.py:160
  127.4 1.7 %copy.10 = f32[32,2,512]{2,1,0:T(2,128)} copy(f32[32,2,512]{2,0,1:T(8,128)} %bitcast.5) | data formatting | bytes 262144 | tf_op jit(solution)/shard_map/transpose | solution.py:161
Async XLA Ops:
  6.5 43.7 %all-gather.2.cloned.1.call-start = ((), (), s32[]{:S(2)}) async-start(), calls=%async_computation.1 | async-start | bytes 1114112 | tf_op jit(solution)/shard_map/all_gather | solution.py:151
  8.1 119.2 %reduce-scatter.2.cloned.1.call-start = ((), (), s32[]{:S(2)}) async-start(), calls=%async_computation.2 | async-start | bytes 2228224 | tf_op jit(solution)/shard_map/reduce_scatter | solution.py:160
Sparse Core Ops, SparseCore 0:
  9.5 40.6 all-gather.1
  66.9 60.4 reduce-scatter.1

commit v2 on v1

v2 whole, which is shorter than its diff:
```python
import functools

import jax
import jax.numpy as jnp
from jax import lax
from jax.experimental import pallas as pl
from jax.experimental.pallas import tpu as pltpu
from jax.sharding import PartitionSpec as P

BLOCK = 128
EDGE = 16
F32 = jnp.float32
BF16 = jnp.bfloat16


def dot(a, b):
    return jnp.dot(a, b, preferred_element_type=F32)


def build_bands(taps_ref, plain_ref, flipped_ref, shift, place):
    taps = taps_ref[...].astype(F32)
    bases, width = taps.shape
    half = width // 2
    extent = plain_ref.shape[1]
    blocks = extent // BLOCK
    zero = jnp.zeros((extent, extent), plain_ref.dtype)
    for k in range(bases):
        plain_ref[k] = zero
        flipped_ref[k] = zero

    for first, rows, aside in ((0, BLOCK, 0), (0, EDGE, -1), (BLOCK - EDGE, EDGE, 1)):
        shape = (rows, BLOCK)
        row = lax.broadcasted_iota(jnp.int32, shape, 0) + first
        column = lax.broadcasted_iota(jnp.int32, shape, 1) + aside * BLOCK
        ahead = row - column + (half - shift)
        behind = column - row + (half - shift)
        plain = [jnp.zeros(shape, F32) for _ in range(bases)]
        flipped = [jnp.zeros(shape, F32) for _ in range(bases)]
        for t in range(width):
            match_ahead = ahead == t
            match_behind = behind == t
            for k in range(bases):
                tap = taps[k : k + 1, t : t + 1]
                plain[k] = jnp.where(match_ahead, tap, plain[k])
                flipped[k] = jnp.where(match_behind, tap, flipped[k])
        for block in range(blocks):
            if not 0 <= block + aside < blocks:
                continue
            source = row + (block * BLOCK - shift)
            target = column + (block * BLOCK - shift)
            row_inside = (source >= 0) & (source < extent)
            column_inside = (target >= 0) & (target < extent)
            outer_row = block in (0, blocks - 1)
            outer_column = block + aside in (0, blocks - 1)
            columns = pl.ds((block + aside) * BLOCK, BLOCK)
            for k in range(bases):
                one = jnp.where(row_inside, plain[k], 0.0) if outer_row else plain[k]
                two = jnp.where(column_inside, flipped[k], 0.0) if outer_column else flipped[k]
                one, two = one.astype(BF16), two.astype(BF16)
                flipped_ref[k, pl.ds(block * BLOCK + first, rows), columns] = two
                for piece in range(0, rows, EDGE):
                    to = place(block * BLOCK + first + piece)
                    plain_ref[k, pl.ds(to, EDGE), columns] = one[piece : piece + EDGE]


def forward_residual(estimate, patch, observed, mask, spread, row_band, column_flip, model):
    def basis(k, _):
        rowed = dot(estimate[patch], row_band[k]).astype(BF16)
        model[...] += mix_full(spread, k) * dot(column_flip[k], rowed)
        return 0

    model[...] = jnp.zeros_like(model)
    lax.fori_loop(0, row_band.shape[0], basis, 0)
    model[...] = mask[0].astype(F32) * (model[...] - observed[0].astype(F32))


def backward(first, last, make, rows, spread, row_flip, column_band, model, weighted, total):
    def basis(k, _):
        if make:
            weighted[k] = (mix_full(spread, k) * model[...]).astype(BF16)
        backed = dot(column_band[k, rows, :], weighted[k]).astype(BF16)
        total[...] += dot(backed, row_flip[k])
        return 0

    lax.fori_loop(first, last, basis, 0)


def local_kernel(
    dithers, patch_of, estimate, observed, mask, mix, column_taps, row_taps, term,
    row_band, row_flip, column_band, column_flip, spread, weighted, model, total,
):
    extent = observed.shape[1]
    build_bands(row_taps, row_band, row_flip, dithers[0, 1], lambda r: r)
    build_bands(column_taps, column_band, column_flip, dithers[0, 0], lambda r: r)
    spread_mix(mix, spread)
    patch = patch_of[0]
    forward_residual(estimate, patch, observed, mask, spread, row_band, column_flip, model)
    bases = spread.shape[0]
    total[...] = jnp.zeros_like(total)
    everything = pl.ds(0, extent)
    backward(0, bases, True, everything, spread, row_flip, column_band, model, weighted, total)
    for q in range(term.shape[0]):
        term[q] = jnp.where(patch == q, total[...], 0.0)


def fused_kernel(
    size, dithers, patch_of, estimate, observed, mask, mix, column_taps, row_taps, out,
    row_band, row_flip, column_band, column_flip, spread, weighted, model, total,
    gathered, low, from_core, to_row, from_row, to_plane, from_plane,
    z_send, z_recv, y_send, y_recv, c_send, c_recv,
    rc_send, rc_recv, ry_send, ry_recv, rz_send, rz_recv,
):
    planes = size // 4
    band, patches, _ = estimate.shape
    extent = observed.shape[1]
    bases = spread.shape[0]
    quarter = extent // 4
    me = lax.axis_index("exp")
    plane, y, core = me // 4, (me // 2) % 2, me % 2

    def index(p, yy, cc):
        return p * 4 + yy * 2 + cc

    def ahead(d):
        return lax.rem(plane + d, planes)

    def behind(d):
        return lax.rem(plane + planes - d, planes)

    other_core, other_row = index(plane, y, 1 - core), index(plane, 1 - y, core)

    def copy(source, target, send, recv, device):
        return pltpu.make_async_remote_copy(
            src_ref=source, dst_ref=target, send_sem=send, recv_sem=recv,
            device_id={"exp": device}, device_id_type=pl.DeviceIdType.MESH,
        )

    def shard(owner):
        return gathered.at[:, pl.ds(pl.multiple_of(owner * band, band), band), :]

    def rows_at(start, count):
        return pl.ds(pl.multiple_of(start, count), count)

    barrier = pltpu.get_barrier_semaphore()
    partners = [other_core, other_row] + [index(ahead(d), y, core) for d in range(1, planes)]
    for partner in partners:
        pl.semaphore_signal(
            barrier, inc=1, device_id={"exp": partner}, device_id_type=pl.DeviceIdType.MESH
        )
    mine = rows_at(me * band, band)
    for q in range(patches):
        gathered[q, mine, :] = estimate[:, q, :].astype(BF16)
    pl.semaphore_wait(barrier, len(partners))

    def z_copy(d):
        return copy(shard(me), shard(me), z_send.at[d], z_recv.at[d], index(ahead(d), y, core))

    def y_copy(d):
        held = shard(index(behind(d), y, core))
        return copy(held, held, y_send.at[d], y_recv.at[d], other_row)

    def c_copy(d, across):
        held = shard(index(behind(d), (1 - y) if across else y, core))
        slot = d * 2 + across
        return copy(held, held, c_send.at[slot], c_recv.at[slot], other_core)

    for d in range(1, planes):
        z_copy(d).start()
    y_copy(0).start()
    c_copy(0, 0).start()
    build_bands(row_taps, row_band, row_flip, dithers[0, 1], lambda r: r)
    for d in range(1, planes):
        z_copy(d).wait_recv()
        y_copy(d).start()
        c_copy(d, 0).start()

    def place(r):
        owner, within = r // band, r % band
        p, yy, cc = owner // 4, (owner // 2) % 2, owner % 2
        return ((yy * 2 + cc) * planes + p) * band + within

    build_bands(column_taps, column_band, column_flip, dithers[0, 0], place)
    spread_mix(mix, spread)
    for d in range(planes):
        y_copy(d).wait_recv()
        c_copy(d, 1).start()
    for d in range(planes):
        for across in (0, 1):
            c_copy(d, across).wait_recv()

    patch = patch_of[0]
    forward_residual(gathered, patch, observed, mask, spread, row_band, column_flip, model)

    def share(yy, cc):
        return low.at[:, rows_at((yy * 2 + cc) * quarter, quarter), :]

    def finish(yy):
        half = rows_at(yy * 2 * quarter, 2 * quarter)
        for q in range(patches):
            low[q, half, :] = jnp.where(patch == q, total[...], 0.0).astype(BF16)

    def rc_copy(slot, yy):
        return copy(
            share(yy, 1 - core), from_core.at[slot], rc_send.at[slot], rc_recv.at[slot], other_core
        )

    def piece(ref, p):
        return ref.at[:, rows_at(p * band, band), :]

    def ry_copy(d):
        p = ahead(d)
        return copy(piece(to_row, p), piece(from_row, p), ry_send.at[d], ry_recv.at[d], other_row)

    def rz_copy(d):
        return copy(
            to_plane.at[d], from_plane.at[d], rz_send.at[d], rz_recv.at[d],
            index(ahead(d), y, core),
        )

    def back(first, last, make, yy):
        half = rows_at(yy * 2 * quarter, 2 * quarter)
        backward(first, last, make, half, spread, row_flip, column_band, model, weighted, total)

    order = list(range(1, planes)) + [0]
    total[...] = jnp.zeros_like(total)
    back(0, bases, True, 1 - y)
    finish(1 - y)
    rc_copy(0, 1 - y).start()
    total[...] = jnp.zeros_like(total)
    back(0, bases // 2, False, y)
    rc_copy(0, 1 - y).wait_recv()
    own = rows_at(((1 - y) * 2 + core) * quarter, quarter)
    for q in range(patches):
        to_row[q] = (low[q, own, :].astype(F32) + from_core[0, q].astype(F32)).astype(BF16)
    for d in order:
        ry_copy(d).start()
    back(bases // 2, bases, False, y)
    finish(y)
    rc_copy(1, y).start()
    rc_copy(1, y).wait_recv()

    def summed(d, q):
        p = ahead(d)
        rows = rows_at((y * 2 + core) * quarter + p * band, band)
        arrived = rows_at(p * band, band)
        return (
            low[q, rows, :].astype(F32)
            + from_core[1, q, arrived, :].astype(F32)
            + from_row[q, arrived, :].astype(F32)
        )

    for d in range(1, planes):
        ry_copy(d).wait_recv()
        for q in range(patches):
            to_plane[d, q] = summed(d, q).astype(BF16)
        rz_copy(d).start()
    ry_copy(0).wait_recv()
    final = [summed(0, q) for q in range(patches)]
    for d in range(1, planes):
        rz_copy(d).wait_recv()
        for q in range(patches):
            final[q] = final[q] + from_plane[d, q].astype(F32)
    for q in range(patches):
        out[:, q, :] = final[q]

    for d in range(planes):
        if d > 0:
            z_copy(d).wait_send()
            rz_copy(d).wait_send()
        y_copy(d).wait_send()
        c_copy(d, 0).wait_send()
        c_copy(d, 1).wait_send()
        ry_copy(d).wait_send()
    rc_copy(0, 1 - y).wait_send()
    rc_copy(1, y).wait_send()


def work_shapes(bases, tiles, extent, total_rows):
    return [pltpu.VMEM((bases, extent, extent), BF16) for _ in range(4)] + [
        pltpu.VMEM((bases, tiles, extent), F32),
        pltpu.VMEM((bases, extent, extent), BF16),
        pltpu.VMEM((extent, extent), F32),
        pltpu.VMEM((total_rows, extent), F32),
    ]


def per_device(
    size, estimate, observed, pixel_mask, blur_mix, dithers, patch_of, column_taps, row_taps
):
    extent = observed.shape[1]
    band, patches, _ = estimate.shape
    bases, tiles = blur_mix.shape[1:3]
    vmem = pl.BlockSpec(memory_space=pltpu.VMEM)
    smem = pl.BlockSpec(memory_space=pltpu.SMEM)
    in_specs = [smem, smem] + [vmem] * 6
    limit = 56 * 2**20
    if size % 4 == 0 and size >= 8 and band % EDGE == 0:
        planes, quarter = size // 4, extent // 4
        sems = [planes, planes, planes, planes, 2 * planes, 2 * planes, 2, 2] + [planes] * 4
        return pl.pallas_call(
            functools.partial(fused_kernel, size),
            out_shape=jax.ShapeDtypeStruct(estimate.shape, F32),
            in_specs=in_specs,
            out_specs=vmem,
            scratch_shapes=work_shapes(bases, tiles, extent, extent // 2)
            + [
                pltpu.VMEM((patches, extent, extent), BF16),
                pltpu.VMEM((patches, extent, extent), BF16),
                pltpu.VMEM((2, patches, quarter, extent), BF16),
                pltpu.VMEM((patches, quarter, extent), BF16),
                pltpu.VMEM((patches, quarter, extent), BF16),
                pltpu.VMEM((planes, patches, band, extent), BF16),
                pltpu.VMEM((planes, patches, band, extent), BF16),
            ]
            + [pltpu.SemaphoreType.DMA((count,)) for count in sems],
            compiler_params=pltpu.CompilerParams(
                collective_id=0, has_side_effects=True, vmem_limit_bytes=limit
            ),
        )(dithers, patch_of, estimate, observed, pixel_mask, blur_mix, column_taps, row_taps)

    low = jnp.transpose(estimate.astype(BF16), (1, 0, 2))
    gathered = lax.all_gather(low, "exp", axis=1, tiled=True)
    term = pl.pallas_call(
        local_kernel,
        out_shape=jax.ShapeDtypeStruct((patches, extent, extent), F32),
        in_specs=in_specs,
        out_specs=vmem,
        scratch_shapes=work_shapes(bases, tiles, extent, extent),
        compiler_params=pltpu.CompilerParams(vmem_limit_bytes=limit),
    )(dithers, patch_of, gathered, observed, pixel_mask, blur_mix, column_taps, row_taps)
    mine = lax.psum_scatter(term, "exp", scatter_dimension=1, tiled=True)
    return jnp.transpose(mine, (1, 0, 2))


def spread_mix(mix_ref, spread_ref):
    _, bases, tiles, _ = mix_ref.shape
    extent = spread_ref.shape[2]
    lane_tile = lax.broadcasted_iota(jnp.int32, (tiles, extent), 1) // (extent // tiles)
    for k in range(bases):
        weights = mix_ref[0, k]
        spread = jnp.zeros((tiles, extent), F32)
        for tile in range(tiles):
            spread = jnp.where(lane_tile == tile, weights[:, tile : tile + 1], spread)
        spread_ref[k] = spread


def mix_full(spread_ref, k):
    tiles, extent = spread_ref.shape[1:]
    weights = spread_ref[k]
    return jnp.broadcast_to(weights[:, None, :], (tiles, extent // tiles, extent)).reshape(
        extent, extent
    )


def solution(mesh):
    in_specs = (
        P("exp", "groups", None),
        P(("groups", "exp"), None, None),
        P(("groups", "exp"), None, None),
        P(("groups", "exp"), None, None, None),
        P(("groups", "exp"), None),
        P(("groups", "exp")),
        P(),
        P(),
    )
    return jax.shard_map(
        functools.partial(per_device, mesh.shape["exp"]),
        mesh=mesh,
        in_specs=in_specs,
        out_specs=P("exp", "groups", None),
        check_vma=False,
    )
```

time: 136 us -> 42.4 us (0.31)
  waiting for transfers between devices: 102 us -> 0 us
  Pallas kernels: 16.5 us -> 40 us
  between operations: 14 us -> 0.66 us
  local copies, waits for them, and re-layouts: 3.22 us -> 1.57 us
    reduce_scatter x1 -> x0, waiting for transfers between devices: 60.6 us -> none  [per_device(): mine = lax.psum_scatter(term, 'exp', scatter_dimension=1, tiled=True)]
    all_gather x1 -> x0, waiting for transfers between devices: 41.4 us -> none  [per_device(): gathered = lax.all_gather(low, 'exp', axis=1, tiled=True)]
    pallas_call x1, Pallas kernels: 16.5 us -> 40 us  [per_device(): pl.pallas_call(functools.partial(fused_kernel, size), out_shape=jax.Shape...]
    transpose x1 -> x0, local copies, waits for them, and re-layouts: 1.66 us -> none  [per_device(): return jnp.transpose(mine, (1, 0, 2))]
  transfers between devices with their start and end apart: 2 -> 0, of which waited for: 2 -> 0; matrix products, arithmetic and copies ran while one was open for 0% -> 0% of each run, Pallas kernels for 0% -> 0%
where the time goes in v2:
time: 42.4 us; the launch traced here: 42.3 us
  Pallas kernels  40 us (94%)
  local copies, waits for them, and re-layouts  1.57 us (4%)
  between operations  0.66 us (2%)
    pallas_call x1, Pallas kernels, per_device(): pl.pallas_call(functools.partial(fused_kernel, size), out_shape=jax.Shape...  40 us
    unnamed x1, local copies, waits for them, and re-layouts  1.57 us

profile of v2, /device:TPU:0, one launch (start us, length us, event | category | flops | bytes accessed | tf_op | source)
XLA Modules:
  0.0 42.3 jit_solution(9420006995056692902)
XLA Ops:
  0.7 40.0 %shard_map.82 = f32[32,2,512]{2,1,0:T(2,128)} custom-call(s32[1,2]{1,0:T(1,128)} %dithers.1, s32[1]{0:T(128)S(6)} %copy.10.patch_of, f32[32,2,512]{2,1,0:T(2,128)} %estimate.1, bf16[1,512,512]{2,1,0:T(8,128)(2,1)} %observed.1, s32[1,512,512]{2,1,0:T(8,128)} %mask.1, f32[1,6,8,8]{3,2,1,0:T(8,128)} %mix.1, bf16[6,15]{1,0:T(8,128)(2,1)} %column_taps.1, ...), custom_call_target="tpu_custom_call" | custom-call | tf_op jit(solution)/shard_map/pallas_call | solution.py:300
  40.7 1.6 %copy.11 = f32[32,2,512]{2,1,0:T(2,128)} copy(f32[32,2,512]{2,1,0:T(2,128)} %shard_map.82) | data formatting | bytes 262144

commit v3 on v2

--- a/solution.py
+++ b/solution.py
@@ -63,15 +63,16 @@
                     plain_ref[k, pl.ds(to, EDGE), columns] = one[piece : piece + EDGE]
 
 
-def forward_residual(estimate, patch, observed, mask, spread, row_band, column_flip, model):
+def forward_residual(observed, mask, spread, column_flip, rowed, model):
+    bases = spread.shape[0]
+    model[...] = mix_full(spread, 0) * dot(column_flip[0], rowed[0])
+
     def basis(k, _):
-        rowed = dot(estimate[patch], row_band[k]).astype(BF16)
-        model[...] += mix_full(spread, k) * dot(column_flip[k], rowed)
+        model[...] += mix_full(spread, k) * dot(column_flip[k], rowed[k])
         return 0
 
-    model[...] = jnp.zeros_like(model)
-    lax.fori_loop(0, row_band.shape[0], basis, 0)
-    model[...] = mask[0].astype(F32) * (model[...] - observed[0].astype(F32))
+    lax.fori_loop(1, bases, basis, 0, unroll=True)
+    model[...] = mask[...].astype(F32) * (model[...] - observed[...].astype(F32))
 
 
 def backward(first, last, make, rows, spread, row_flip, column_band, model, weighted, total):
@@ -82,7 +83,7 @@
         total[...] += dot(backed, row_flip[k])
         return 0
 
-    lax.fori_loop(first, last, basis, 0)
+    lax.fori_loop(first, last, basis, 0, unroll=True)
 
 
 def local_kernel(
@@ -94,8 +95,10 @@
     build_bands(column_taps, column_band, column_flip, dithers[0, 0], lambda r: r)
     spread_mix(mix, spread)
     patch = patch_of[0]
-    forward_residual(estimate, patch, observed, mask, spread, row_band, column_flip, model)
     bases = spread.shape[0]
+    for k in range(bases):
+        weighted[k] = dot(estimate[patch], row_band[k]).astype(BF16)
+    forward_residual(observed.at[0], mask.at[0], spread, column_flip, weighted, model)
     total[...] = jnp.zeros_like(total)
     everything = pl.ds(0, extent)
     backward(0, bases, True, everything, spread, row_flip, column_band, model, weighted, total)
@@ -108,7 +111,7 @@
     row_band, row_flip, column_band, column_flip, spread, weighted, model, total,
     gathered, low, from_core, to_row, from_row, to_plane, from_plane,
     z_send, z_recv, y_send, y_recv, c_send, c_recv,
-    rc_send, rc_recv, ry_send, ry_recv, rz_send, rz_recv,
+    rc_send, rc_recv, ry_send, ry_recv, rz_send, rz_recv, frame, good, load_sem,
 ):
     planes = size // 4
     band, patches, _ = estimate.shape
@@ -141,6 +144,10 @@
     def rows_at(start, count):
         return pl.ds(pl.multiple_of(start, count), count)
 
+    loads = [
+        pltpu.make_async_copy(observed.at[0], frame, load_sem.at[0]),
+        pltpu.make_async_copy(mask.at[0], good, load_sem.at[1]),
+    ]
     barrier = pltpu.get_barrier_semaphore()
     partners = [other_core, other_row] + [index(ahead(d), y, core) for d in range(1, planes)]
     for partner in partners:
@@ -164,10 +171,12 @@
         slot = d * 2 + across
         return copy(held, held, c_send.at[slot], c_recv.at[slot], other_core)
 
+    y_copy(0).start()
     for d in range(1, planes):
         z_copy(d).start()
-    y_copy(0).start()
     c_copy(0, 0).start()
+    for load in loads:
+        load.start()
     build_bands(row_taps, row_band, row_flip, dithers[0, 1], lambda r: r)
     for d in range(1, planes):
         z_copy(d).wait_recv()
@@ -179,29 +188,57 @@
         p, yy, cc = owner // 4, (owner // 2) % 2, owner % 2
         return ((yy * 2 + cc) * planes + p) * band + within
 
+    def forward_y(d):
+        y_copy(d).wait_recv()
+        c_copy(d, 1).start()
+
+    def blur_rows(yy):
+        starts = [p * 4 * band + yy * 2 * band for p in range(planes)]
+
+        def of_patch(q):
+            return jnp.concatenate(
+                [gathered[q, rows_at(start, 2 * band), :] for start in starts], axis=0
+            )
+
+        joined = of_patch(0)
+        for q in range(1, patches):
+            joined = jnp.where(patch == q, of_patch(q), joined)
+        for k in range(bases):
+            rowed = dot(joined, row_band[k]).astype(BF16)
+            for p in range(planes):
+                piece_rows = rowed[p * 2 * band : (p + 1) * 2 * band]
+                weighted[k, rows_at(starts[p], 2 * band), :] = piece_rows
+
+    patch = patch_of[0]
+    forward_y(0)
     build_bands(column_taps, column_band, column_flip, dithers[0, 0], place)
     spread_mix(mix, spread)
+    forward_y(1)
     for d in range(planes):
-        y_copy(d).wait_recv()
-        c_copy(d, 1).start()
+        c_copy(d, 0).wait_recv()
+    blur_rows(y)
+    for d in range(2, planes):
+        forward_y(d)
     for d in range(planes):
-        for across in (0, 1):
-            c_copy(d, across).wait_recv()
-
-    patch = patch_of[0]
-    forward_residual(gathered, patch, observed, mask, spread, row_band, column_flip, model)
-
-    def share(yy, cc):
-        return low.at[:, rows_at((yy * 2 + cc) * quarter, quarter), :]
+        c_copy(d, 1).wait_recv()
+    blur_rows(1 - y)
+    for load in loads:
+        load.wait()
+    forward_residual(frame, good, spread, column_flip, weighted, model)
 
     def finish(yy):
         half = rows_at(yy * 2 * quarter, 2 * quarter)
         for q in range(patches):
             low[q, half, :] = jnp.where(patch == q, total[...], 0.0).astype(BF16)
 
-    def rc_copy(slot, yy):
+    def rc_copy(slot, d):
+        yy = y if slot else 1 - y
+        p = ahead(d)
+        at = slot * planes + d
+        rows = rows_at((yy * 2 + 1 - core) * quarter + p * band, band)
         return copy(
-            share(yy, 1 - core), from_core.at[slot], rc_send.at[slot], rc_recv.at[slot], other_core
+            low.at[:, rows, :], from_core.at[slot, :, rows_at(p * band, band), :],
+            rc_send.at[at], rc_recv.at[at], other_core,
         )
 
     def piece(ref, p):
@@ -225,19 +262,23 @@
     total[...] = jnp.zeros_like(total)
     back(0, bases, True, 1 - y)
     finish(1 - y)
-    rc_copy(0, 1 - y).start()
+    for d in order:
+        rc_copy(0, d).start()
     total[...] = jnp.zeros_like(total)
     back(0, bases // 2, False, y)
-    rc_copy(0, 1 - y).wait_recv()
-    own = rows_at(((1 - y) * 2 + core) * quarter, quarter)
-    for q in range(patches):
-        to_row[q] = (low[q, own, :].astype(F32) + from_core[0, q].astype(F32)).astype(BF16)
     for d in order:
+        rc_copy(0, d).wait_recv()
+        p = ahead(d)
+        own = rows_at(((1 - y) * 2 + core) * quarter + p * band, band)
+        arrived = rows_at(p * band, band)
+        for q in range(patches):
+            both = low[q, own, :].astype(F32) + from_core[0, q, arrived, :].astype(F32)
+            to_row[q, arrived, :] = both.astype(BF16)
         ry_copy(d).start()
     back(bases // 2, bases, False, y)
     finish(y)
-    rc_copy(1, y).start()
-    rc_copy(1, y).wait_recv()
+    for d in order:
+        rc_copy(1, d).start()
 
     def summed(d, q):
         p = ahead(d)
@@ -250,10 +291,12 @@
         )
 
     for d in range(1, planes):
+        rc_copy(1, d).wait_recv()
         ry_copy(d).wait_recv()
         for q in range(patches):
             to_plane[d, q] = summed(d, q).astype(BF16)
         rz_copy(d).start()
+    rc_copy(1, 0).wait_recv()
     ry_copy(0).wait_recv()
     final = [summed(0, q) for q in range(patches)]
     for d in range(1, planes):
@@ -271,8 +314,8 @@
         c_copy(d, 0).wait_send()
         c_copy(d, 1).wait_send()
         ry_copy(d).wait_send()
-    rc_copy(0, 1 - y).wait_send()
-    rc_copy(1, y).wait_send()
+        rc_copy(0, d).wait_send()
+        rc_copy(1, d).wait_send()
 
 
 def work_shapes(bases, tiles, extent, total_rows):
@@ -296,11 +339,11 @@
     limit = 56 * 2**20
     if size % 4 == 0 and size >= 8 and band % EDGE == 0:
         planes, quarter = size // 4, extent // 4
-        sems = [planes, planes, planes, planes, 2 * planes, 2 * planes, 2, 2] + [planes] * 4
+        sems = [planes, planes, planes, planes, 2 * planes, 2 * planes] + [2 * planes] * 2 + [planes] * 4
         return pl.pallas_call(
             functools.partial(fused_kernel, size),
             out_shape=jax.ShapeDtypeStruct(estimate.shape, F32),
-            in_specs=in_specs,
+            in_specs=[smem, smem, vmem] + [pl.BlockSpec(memory_space=pl.ANY)] * 2 + [vmem] * 3,
             out_specs=vmem,
             scratch_shapes=work_shapes(bases, tiles, extent, extent // 2)
             + [
@@ -312,7 +355,12 @@
                 pltpu.VMEM((planes, patches, band, extent), BF16),
                 pltpu.VMEM((planes, patches, band, extent), BF16),
             ]
-            + [pltpu.SemaphoreType.DMA((count,)) for count in sems],
+            + [pltpu.SemaphoreType.DMA((count,)) for count in sems]
+            + [
+                pltpu.VMEM((extent, extent), observed.dtype),
+                pltpu.VMEM((extent, extent), pixel_mask.dtype),
+                pltpu.SemaphoreType.DMA((2,)),
+            ],
             compiler_params=pltpu.CompilerParams(
                 collective_id=0, has_side_effects=True, vmem_limit_bytes=limit
             ),

time: 42.4 us -> 38.6 us (0.910)
  Pallas kernels: 40 us -> 36.3 us
    pallas_call x1, Pallas kernels: 40 us -> 36.3 us  [per_device(): pl.pallas_call(functools.partial(fused_kernel, size), out_shape=jax.Shape...]
where the time goes in v3:
time: 38.6 us; the launch traced here: 38.5 us
  Pallas kernels  36.3 us (94%)
  local copies, waits for them, and re-layouts  1.57 us (4%)
  between operations  0.66 us (2%)
    pallas_call x1, Pallas kernels, per_device(): pl.pallas_call(functools.partial(fused_kernel, size), out_shape=jax.Shape...  36.3 us
    unnamed x1, local copies, waits for them, and re-layouts  1.57 us

profile of v3, /device:TPU:0, one launch (start us, length us, event | category | flops | bytes accessed | tf_op | source)
XLA Modules:
  0.0 38.5 jit_solution(7857049847875235870)
XLA Ops:
  0.7 36.3 %shard_map.82 = f32[32,2,512]{2,1,0:T(2,128)} custom-call(s32[1,2]{1,0:T(1,128)} %dithers.1, s32[1]{0:T(128)S(6)} %copy.10.patch_of, f32[32,2,512]{2,1,0:T(2,128)} %estimate.1, bf16[1,512,512]{2,1,0:T(8,128)(2,1)} %observed.1, s32[1,512,512]{2,1,0:T(8,128)} %mask.1, f32[1,6,8,8]{3,2,1,0:T(8,128)} %mix.1, bf16[6,15]{1,0:T(8,128)(2,1)} %column_taps.1, ...), custom_call_target="tpu_custom_call" | custom-call | tf_op jit(solution)/shard_map/pallas_call | solution.py:343
  36.9 1.6 %copy.11 = f32[32,2,512]{2,1,0:T(2,128)} copy(f32[32,2,512]{2,1,0:T(2,128)} %shard_map.82) | data formatting | bytes 262144
